TPU v7x, 512 devices: a whole 4x4x16 slice. The times are simulated.
512 devices in a mesh: blk: 16 (over z_hi, x, core), tm: 32 (over z_lo, y).
Axes of the slice: x: 4, y: 4, z: 16 (z_hi: 2, z_lo: 8; z = z_hi * 8 + z_lo), core: 2. Of those that a mesh axis runs over, the one named last changes fastest.
Arguments:
- waveform: bfloat16 [400, 3, 20480], P('blk', None, 'tm'), may hold values from -600 to 600
- templates: bfloat16 [64, 12, 3, 600], P('blk'), may hold values from -6 to 6
- station_index: int32 [64, 12], P('blk'), may hold values from 0 to 399, as said below
- channel_mask: int32 [64, 12, 3], P('blk'), may hold values from 0 to 1, as said below
Outputs:
- detection: float32 [64, 20480], P('blk', 'tm')
Inputs may be any that keep to these rules, and one draw needn't show every extreme that they name: `station_index`: each template names 12 different stations. `channel_mask`: every template station has at least one used component.
All inputs are finite; a program needn't handle non-finite values.
Results may differ from a plain program's by a relative error of at most 0.0003.
Values may be sent and summed in bfloat16 or wider, within the bound.
A program may use at most 192 MiB of HBM per device.

v0:
```python
import math

import jax
import jax.numpy as jnp
from jax import lax
from jax.sharding import PartitionSpec as P

floor_share = 0.25
epsilon = 1e-06


def from_behind(block, axis, distance):
    devices = range(lax.axis_size(axis))
    route = [(i - distance, i) for i in devices if i - distance in devices]
    return lax.ppermute(block, axis, route)


def window_energy(extended, tpl_width):
    squared = jnp.square(extended.astype(jnp.float32))
    running = jnp.cumsum(squared, axis=2)
    leading = jnp.zeros(running.shape[:2] + (1,), jnp.float32)
    running = jnp.concatenate([leading, running], axis=2)
    return running[:, :, tpl_width:] - running[:, :, :-tpl_width]


def stack_block(extended, scales, shapes_block, rows_block, mask_block):
    members, subset, channels, tpl_width = shapes_block.shape
    time_len = scales.shape[2]
    block_len = math.gcd(time_len, 128)
    span_len = tpl_width + block_len - 1
    block_count = time_len // block_len
    lane_count = members * subset * channels
    traces = jnp.take(extended, rows_block, axis=0).reshape(lane_count, extended.shape[2])
    shapes_flat = shapes_block.reshape(lane_count, tpl_width)
    offsets = (
        jnp.arange(span_len, dtype=jnp.int32)[:, None]
        - jnp.arange(block_len, dtype=jnp.int32)[None, :]
    )
    inside = (offsets >= 0) & (offsets < tpl_width)
    lookup = jnp.clip(offsets, 0, tpl_width - 1)
    toeplitz = jnp.where(
        inside[None], jnp.take(shapes_flat, lookup, axis=1), jnp.zeros((), shapes_flat.dtype)
    )
    starts = (
        jnp.arange(block_count, dtype=jnp.int32)[:, None] * block_len
        + jnp.arange(span_len, dtype=jnp.int32)[None, :]
    )
    windows = jnp.take(traces, starts, axis=1)
    correlation = jnp.einsum("knu,kui->kni", windows, toeplitz, preferred_element_type=jnp.float32)
    correlation = correlation.reshape(members, subset, channels, time_len)
    template_norm = lax.rsqrt(
        jnp.einsum("kjcl,kjcl->kjc", shapes_block, shapes_block, preferred_element_type=jnp.float32)
        + epsilon
    )
    live_mask = mask_block.astype(jnp.float32)
    weights = template_norm * live_mask
    window_norms = jnp.take(scales, rows_block, axis=0)
    summed = jnp.sum(correlation * window_norms * weights[..., None], axis=(1, 2))
    counts = jnp.sum(live_mask, axis=(1, 2))
    return summed * jnp.sqrt(tpl_width / counts)[:, None]


def per_device(waveform, templates, station_index, channel_mask):
    tpl_width = templates.shape[3]
    lag_reach = tpl_width - 1
    gathered = lax.all_gather(waveform, "blk", axis=0, tiled=True)
    border = from_behind(gathered[:, :, :lag_reach], "tm", -1)
    extended = jnp.concatenate([gathered, border], axis=2)
    energy = window_energy(extended, tpl_width)
    scales = lax.rsqrt(jnp.maximum(energy, floor_share * tpl_width))
    local_count, subset, channels = channel_mask.shape
    members = math.gcd(local_count, 4)
    blocks = local_count // members

    def one_block(group_items):
        return stack_block(extended, scales, group_items[0], group_items[1], group_items[2])

    stacked = lax.map(
        one_block,
        (
            templates.reshape(blocks, members, subset, channels, tpl_width),
            station_index.reshape(blocks, members, subset),
            channel_mask.reshape(blocks, members, subset, channels),
        ),
    )
    return stacked.reshape(local_count, -1)


def solution(mesh):
    return jax.shard_map(
        per_device,
        mesh=mesh,
        in_specs=(
            P("blk", None, "tm"),
            P("blk", None, None, None),
            P("blk", None),
            P("blk", None, None),
        ),
        out_specs=P("blk", "tm"),
        check_vma=False,
    )
```

profile of v0, /device:TPU:24, one launch (start us, length us, event | category | flops | bytes accessed | tf_op | source)
XLA Modules:
  0.0 603.0 jit_solution(1696981378589394115)
XLA Ops:
  9.7 363.5 %gather_fusion.2 = bf16[93056,144]{1,0:T(8,128)(2,1)} fusion(bf16[144,600]{0,1:T(8,128)(2,1)S(1)} %copy.40, s32[93184]{0:T(1024)S(1)} %pad_clamp_fusion), kind=kCustom, calls=%fused_computation.2 | custom fusion | bytes 53972480 | tf_op jit(solution)/shard_map/while/body/eval_jaxpr/jit(_take)/gather | solution.py:42
  373.1 54.9 %copy.41 = bf16[727,128,144]{1,0,2:T(8,128)(2,1)} copy(bf16[727,128,144]{2,1,0:T(8,128)(2,1)} %bitcast.20) | data formatting | bytes 53600256 | tf_op jit(solution)/shard_map/while/body/eval_jaxpr/jit(_take)/gather | solution.py:42
  430.1 2.7 collective-permute-start
  433.7 2.3 constant_dynamic-update-slice_fusion
  436.0 33.5 %collective-permute-done = bf16[400,3,599]{2,0,1:T(8,128)(2,1)S(1)} collective-permute-done((bf16[400,3,599]{2,0,1:T(8,128)(2,1)S(1)}, bf16[400,3,599]{2,0,1:T(8,128)(2,1)S(1)}, u32[]{:S(2)}, u32[]{:S(2)}) %collective-permute-start) | collective-permute-done | bytes 1437632 | tf_op jit(solution)/shard_map/ppermute | solution.py:15
  470.5 1.9 copy-done.1
  472.4 4.6 convert_multiply_fusion
  476.9 10.6 %copy.55 = f32[400,3,1239]{0,2,1:T(8,128)} copy(f32[400,3,1239]{2,1,0:T(4,128)} %convert_multiply_fusion) | data formatting | bytes 11894400
  487.6 7.4 %pad.4.clone = f32[400,3,1280]{0,2,1:T(8,128)} pad(f32[400,3,1239]{0,2,1:T(8,128)} %copy.55, f32[]{:T(128)} %constant.100.clone.1), padding=0_0x0_0x0_41 | pad | bytes 12091204 | tf_op jit(solution)/shard_map/pad
  495.0 9.6 %fusion.8 = f32[400,3,10,128]{0,2,1,3:T(8,128)S(1)} fusion(f32[400,3,10,128]{0,3,2,1:T(8,128)} %bitcast.23), kind=kOutput, calls=%fused_computation.12 | output fusion | flops 195072000 | bytes 12288000 | tf_op jit(solution)/shard_map/reduce-window
  504.7 4.6 copy-done
  509.3 12.1 %broadcast_add_fusion = f32[400,3,10,128]{0,2,1,3:T(8,128)} fusion(f32[400,3,10,128]{0,2,1,3:T(8,128)} %copy-done, f32[400,3,10]{0,2,1:T(8,128)S(1)} %bitcast.26), kind=kLoop, calls=%fused_computation.16 | loop fusion | flops 1536000 | bytes 12336000 | tf_op jit(solution)/shard_map/reduce_window_sum
  521.4 9.1 %copy.44 = f32[400,3,10,128]{0,3,2,1:T(8,128)S(1)} copy(f32[400,3,10,128]{0,2,1,3:T(8,128)} %broadcast_add_fusion) | data formatting | bytes 12288000 | tf_op jit(solution)/shard_map/reduce_window_sum
  530.6 2.4 slice.36
  533.0 4.0 slice.37
  537.0 3.1 gather_fusion
  540.8 11.3 %gather_fusion.1 = bf16[3635,144]{1,0:T(8,128)(2,1)S(1)} fusion(bf16[144,1239]{0,1:T(8,128)(2,1)S(1)} %broadcast_select_fusion, s32[4096]{0:T(1024)S(1)} %pad_clamp_fusion.1), kind=kCustom, calls=%fused_computation.1 | custom fusion | bytes 2108300 | tf_op jit(solution)/shard_map/while/body/eval_jaxpr/jit(_take)/gather | solution.py:48
  552.1 2.0 copy.38
  554.1 3.2 reshape.186
  557.3 11.6 %fusion = f32[144,5,128]{2,1,0:T(8,128)S(1)} fusion(bf16[727,128,144]{1,0,2:T(8,128)(2,1)} %copy.41, pred[727,128]{1,0:T(8,128)(4,1)S(1)} %get-tuple-element.20, pred[727,128]{1,0:T(8,128)(4,1)S(1)} %get-tuple-element.19, bf16[5,727,144]{1,0,2:T(8,128)(2,1)S(1)} %reshape.186, pred[5,727]{1,0:T(8,128)(4,1)S(1)} %fusion.27), kind=kOutput, calls=%fused_computation.4 | convolution fusion | flops 161324208 | bytes 28405396 | tf_op jit(solution)/shard_map/while/body/eval_jaxpr/knu,kui->kni/dot_general | solution.py:49
  569.1 6.5 %copy.53 = f32[400,3,640]{2,1,0:T(4,128)} copy(f32[400,3,640]{0,2,1:T(8,128)} %slice.36) | data formatting | bytes 6144000
  575.6 10.6 %copy.54 = f32[400,3,1239]{2,1,0:T(4,128)} copy(f32[400,3,1239]{0,2,1:T(8,128)} %slice.37) | data formatting | bytes 11894400
  586.2 5.9 fusion.12
  592.1 3.0 gather_fusion.3
  (44 shorter events, 8.9 us)
Async XLA Ops:
  6.5 421.8 %all-gather.2.cloned.1.call-start = ((), (), s32[]{:S(2)}) async-start(), calls=%async_computation | async-start | bytes 2176000 | tf_op jit(solution)/shard_map/all_gather | solution.py:66
  373.1 54.9 %copy-start.3 = (s32[4,12]{1,0:T(4,128)S(1)}, s32[4,12]{1,0:T(4,128)}, u32[]{:S(2)}) copy-start(s32[4,12]{1,0:T(4,128)} %param.6) | copy-start | bytes 580
  373.1 59.8 %copy-start.2 = (bf16[4,12,3,600]{3,0,2,1:T(4,128)(2,1)S(1)}, bf16[4,12,3,600]{3,0,2,1:T(4,128)(2,1)}, u32[]{:S(2)}) copy-start(bf16[4,12,3,600]{3,0,2,1:T(4,128)(2,1)} %param.5) | copy-start | bytes 518404
  373.1 60.1 %copy-start.4 = (s32[4,12,3]{1,0,2:T(4,128)S(1)}, s32[4,12,3]{1,0,2:T(4,128)}, u32[]{:S(2)}) copy-start(s32[4,12,3]{1,0,2:T(4,128)} %param.7) | copy-start | bytes 1732
  430.1 39.3 %collective-permute-start = (bf16[400,3,599]{2,0,1:T(8,128)(2,1)S(1)}, bf16[400,3,599]{2,0,1:T(8,128)(2,1)S(1)}, u32[]{:S(2)}, u32[]{:S(2)}) collective-permute-start(bf16[400,3,599]{2,0,1:T(8,128)(2,1)S(1)} %copy.35), channel_id=1, source_target_pairs={{1,0},{2,1},{3,2},{4,3},{5,4},{6,5},{7,6},{8,7},{9,8},{10,9},{11,1... | collective-permute-start | bytes 4312808 | tf_op jit(solution)/shard_map/ppermute | solution.py:15
  470.5 1.9 copy-start.1
  504.6 4.6 copy-start
Sparse Core Ops, SparseCore 0:
  10.7 95.7 all-gather.1
where the time goes:
time: 607 us; the launch traced here: 603 us
  local copies, waits for them, and re-layouts  508 us (84%)
  other arithmetic  34 us (6%)
  waiting for transfers between devices  33.5 us (6%)
  between operations  13.6 us (2%)
  matrix products  11.6 us (2%)
    gather x2, local copies, waits for them, and re-layouts, stack_block(): jnp.take(shapes_flat, lookup, axis=1)  418 us
    unnamed x16, local copies, waits for them, and re-layouts  39.2 us
    ppermute x1, waiting for transfers between devices, from_behind(): return lax.ppermute(block, axis, route)  33.5 us
    another operation x3, other arithmetic  21.9 us
    gather x3, local copies, waits for them, and re-layouts, stack_block(): windows = jnp.take(traces, starts, axis=1)  16.5 us
    another operation x3, local copies, waits for them, and re-layouts  13.1 us
  transfers between devices with their start and end apart: 2, of which 1 were waited for; matrix products, arithmetic and copies ran while one was open for 70% of the time, Pallas kernels for 0%

commit v1 on v0

v1 whole, which is shorter than its diff:
```python
import jax
import jax.numpy as jnp
from jax import lax
from jax.experimental import pallas as pl
from jax.experimental.pallas import tpu as pltpu
from jax.sharding import PartitionSpec as P

bf16, f32, i32 = jnp.bfloat16, jnp.float32, jnp.int32
MESH = pl.DeviceIdType.MESH
NT = (((1,), (1,)), ((), ()))

TPL = 600
TIME = 640
PER = 25
ROWS = 80
SUB = 32
LANES = 128
GROUPS = 36
MEMBERS = 4
TRACES = GROUPS * MEMBERS
STREAMS = 4


def build_toeplitz(t_ref, idx_ref, mask_ref, tz, rid, wcol, mcol, first, last):
    def body(g, carry):
        tt = t_ref[pl.ds(2 * g, 2)].astype(f32).reshape(8, TPL)
        norm = lax.rsqrt(jnp.sum(tt * tt, axis=1, keepdims=True) + 1e-6)
        row0 = pl.multiple_of(8 * g, 8)
        wcol[pl.ds(row0, 8), :] = jnp.broadcast_to(norm, (8, LANES))
        padded = jnp.concatenate([tt, jnp.zeros((8, TIME - TPL), f32)], axis=1)
        for i in range(8):
            jc = 2 * g + i // 4
            k = i % 4
            j = jc // 3
            c = jc - 3 * j
            station = idx_ref[k, j]
            owner = station // PER
            row = owner * ROWS + c * PER + (station - PER * owner)
            rid[pl.ds(row0 + i, 1), :] = jnp.full((1, LANES), row, i32)
            mcol[pl.ds(row0 + i, 1), :] = jnp.full((1, LANES), mask_ref[c, k, j].astype(f32), f32)
            base = jnp.broadcast_to(padded[i : i + 1], (SUB, TIME))
            tz[jc, pl.ds(SUB * k, SUB), :] = pltpu.roll(base, 0, 1, stride=1, stride_axis=0).astype(bf16)
        return carry

    lax.fori_loop(first, last, body, 0)


def band_matrix():
    u = lax.broadcasted_iota(i32, (768, LANES), 0)
    b = lax.broadcasted_iota(i32, (768, LANES), 1)
    d = u - b
    return jnp.where((d >= 0) & (d < TPL), 1.0, 0.0).astype(bf16)


def pick_rows(rid, half, blocks, gain):
    ids = jnp.broadcast_to(rid[:, 0:1], (TRACES, 8 * ROWS))
    number = lax.broadcasted_iota(i32, (TRACES, 8 * ROWS), 1) + half * (8 * ROWS)
    chosen = (jnp.where(ids == number, 1.0, 0.0) * gain).astype(bf16)
    return jnp.dot(chosen, blocks.reshape(8 * ROWS, TIME), preferred_element_type=f32)


def spread(xs, wb):
    full = xs[...]
    for a in range(4):
        moved = full if a == 0 else pltpu.roll(full, 2 * TIME - SUB * a, 1)
        for m in range(10):
            wb[pl.ds(4 * m + a, TRACES, stride=40), :] = moved[:, LANES * m : LANES * (m + 1)]


def window_scales(xs, band, wcol, mcol, sc):
    high, low = [], []
    for m in range(10):
        part = xs[:, LANES * m : LANES * (m + 1)]
        square = part * part
        top = square.astype(bf16)
        high.append(top)
        low.append((square - top.astype(f32)).astype(bf16))
    weight = wcol[...] * mcol[...]
    lane = lax.broadcasted_iota(i32, (TRACES, LANES), 1) // SUB
    member = lax.rem(lax.broadcasted_iota(i32, (TRACES, LANES), 0), MEMBERS)
    for a in range(5):
        energy = jnp.dot(jnp.concatenate(high[a : a + 6], axis=1), band, preferred_element_type=f32)
        energy += jnp.dot(jnp.concatenate(low[a : a + 6], axis=1), band, preferred_element_type=f32)
        scale = lax.rsqrt(jnp.maximum(energy, 0.25 * TPL)) * weight
        turned = [scale] + [pltpu.roll(scale, SUB * d, 1) for d in range(1, 4)]
        for a2 in range(4):
            v = jnp.zeros((TRACES, LANES), f32)
            for k in range(MEMBERS):
                v = jnp.where((lane == k) & (member == k), turned[(k - a2) % 4], v)
            sc[pl.ds(4 * a + a2, TRACES, stride=24), :] = v


def correlate(tz, wb, sc, unroll=6):
    def body(g, acc):
        for q in range(unroll):
            jc = g * unroll + q
            parts = []
            for k in range(MEMBERS):
                row = pl.multiple_of((jc * MEMBERS + k) * 40, 8)
                parts.append(jnp.concatenate([wb[pl.ds(row + 4 * p, 24), :] for p in range(5)], axis=1))
            windows = jnp.concatenate(parts, axis=0).astype(bf16)
            c = lax.dot_general(windows, tz[jc], NT, preferred_element_type=f32)
            acc = acc + c * sc[pl.ds(pl.multiple_of(jc * 96, 8), 96), :]
        return acc

    return lax.fori_loop(0, GROUPS // unroll, body, jnp.zeros((96, LANES), f32))


def finish(acc, mcol, accs, o_ref):
    counts = jnp.sum(mcol[...].reshape(GROUPS, MEMBERS, LANES), axis=0)
    factor = jnp.sqrt(TPL / counts)
    accs[...] = acc
    lane = lax.broadcasted_iota(i32, (8, LANES), 1) // SUB
    for k in range(MEMBERS):
        out = jnp.zeros((8, LANES), f32)
        for q in range(4):
            rows = accs[pl.ds(24 * k + q, 5, stride=4), :]
            rows = jnp.concatenate([rows, jnp.zeros((3, LANES), f32)], axis=0)
            if q != k:
                rows = pltpu.roll(rows, (SUB * (q - k)) % LANES, 1)
            out = jnp.where(lane == q, rows, out)
        for m in range(5):
            o_ref[k : k + 1, LANES * m : LANES * (m + 1)] = out[m : m + 1, :] * factor[k : k + 1, :]


def kernel(
    w_ref, t_ref, idx_ref, mask_ref, o_ref,
    gm, gh, relay, tz, rid, wcol, mcol, xs, wb, sc, accs,
    x_send, x_recv, s_send, s_recv, z_send, z_recv, h_send, h_recv,
):
    blk, tm = lax.axis_index("blk"), lax.axis_index("tm")
    zh, x, core = blk // 8, lax.rem(blk // 2, 4), lax.rem(blk, 2)
    zl, y = tm // 4, lax.rem(tm, 4)
    z = zh * 8 + zl
    turn = 1 - 2 * core

    def at_z(to):
        to = lax.rem(to + 32, 16)
        return (lax.div(to, 8) * 8 + x * 2 + core, lax.rem(to, 8) * 4 + y)

    def at_x(to):
        return (zh * 8 + lax.rem(to + 8, 4) * 2 + core, tm)

    ahead, behind = at_x(x + turn), at_x(x - turn)
    sibling = (zh * 8 + x * 2 + 1 - core, tm)
    z_ahead, z_behind = at_z(z + 4 * turn), at_z(z - 4 * turn)
    later, earlier = (blk, lax.rem(tm + 1, 32)), (blk, lax.rem(tm + 31, 32))

    barrier = pltpu.get_barrier_semaphore()
    friends = (ahead, behind, sibling, z_ahead, z_behind, later, earlier)
    for friend in friends:
        pl.semaphore_signal(barrier, inc=1, device_id=friend, device_id_type=MESH)

    own = w_ref[...].astype(f32)
    packed = jnp.concatenate([own[0], own[1], own[2], jnp.zeros((ROWS - 3 * PER, TIME), f32)], axis=0)
    gm[blk] = packed.astype(bf16)
    pl.semaphore_wait(barrier, len(friends))

    def copy(src, dst, send, recv, to):
        return pltpu.make_async_remote_copy(
            src_ref=src, dst_ref=dst, send_sem=send, recv_sem=recv, device_id=to, device_id_type=MESH
        )

    half = [zh, 1 - zh, zh, 1 - zh]
    store = [gm, gm, gh, gh]
    around = [x, x - turn, x + turn, x + 2]

    def slot(s, place, c):
        return store[s].at[half[s] * 8 + lax.rem(place + 8, 4) * 2 + c]

    def x_copy(s, n):
        block = slot(s, around[1] if n == 2 else around[0], core)
        return copy(block, block, x_send.at[s, n], x_recv.at[s, n], behind if n == 1 else ahead)

    def x_wait(s, n):
        place = (x - turn, x + turn, x + 2)[n]
        block = slot(s, place, core)
        copy(block, block, x_send.at[s, n], x_recv.at[s, n], behind).wait_recv()

    def s_copy(s, n):
        block = slot(s, around[n], core)
        return copy(block, block, s_send.at[s, n], s_recv.at[s, n], sibling)

    def s_wait(s, n):
        place = (x, x + turn, x - turn, x + 2)[n]
        block = slot(s, place, 1 - core)
        copy(block, block, s_send.at[s, n], s_recv.at[s, n], sibling).wait_recv()

    mine, theirs = gm.at[blk], gm.at[(1 - zh) * 8 + x * 2 + core]
    z_first = copy(mine, relay, z_send.at[0], z_recv.at[0], z_ahead)
    z_second = copy(relay, gm.at[lax.rem(lax.div(lax.rem(z - 4 * turn + 32, 16), 8), 2) * 8 + x * 2 + core],
                    z_send.at[1], z_recv.at[1], z_ahead)
    z_arrive = copy(relay, theirs, z_send.at[1], z_recv.at[1], z_behind)
    h_copies = [
        copy(mine, gh.at[blk], h_send.at[0], h_recv.at[0], earlier),
        copy(theirs, gh.at[(1 - zh) * 8 + x * 2 + core], h_send.at[1], h_recv.at[1], earlier),
    ]

    def base_ready(s):
        x_copy(s, 0).start()
        x_copy(s, 1).start()
        s_copy(s, 0).start()

    def from_behind(s):
        x_wait(s, 0)
        x_copy(s, 2).start()
        s_copy(s, 1).start()

    def from_ahead(s):
        x_wait(s, 1)
        s_copy(s, 2).start()

    def far(s):
        x_wait(s, 2)
        s_copy(s, 3).start()

    def build(first, last):
        build_toeplitz(t_ref, idx_ref, mask_ref, tz, rid, wcol, mcol, first, last)

    z_first.start()
    h_copies[0].start()
    base_ready(0)
    build(0, 6)
    from_behind(0)
    from_ahead(0)
    h_copies[0].wait_recv()
    base_ready(2)
    z_first.wait_recv()
    z_second.start()
    build(6, 12)
    far(0)
    from_behind(2)
    from_ahead(2)
    build(12, 18)
    far(2)
    for n in range(4):
        s_wait(0, n)
    z_arrive.wait_recv()
    h_copies[1].start()
    base_ready(1)
    xs[:, :TIME] = pick_rows(rid, zh, gm[pl.ds(zh * 8, 8)], 1.0)
    from_behind(1)
    from_ahead(1)
    h_copies[1].wait_recv()
    base_ready(3)
    for n in range(4):
        s_wait(2, n)
    inside = jnp.where(tm < 31, 1.0, 0.0)
    xs[:, TIME:] = pick_rows(rid, zh, gh[pl.ds(zh * 8, 8)], inside)
    far(1)
    from_behind(3)
    from_ahead(3)
    for n in range(4):
        s_wait(1, n)
    xs[:, :TIME] += pick_rows(rid, 1 - zh, gm[pl.ds((1 - zh) * 8, 8)], 1.0)
    band = band_matrix()
    far(3)
    for n in range(4):
        s_wait(3, n)
    xs[:, TIME:] += pick_rows(rid, 1 - zh, gh[pl.ds((1 - zh) * 8, 8)], inside)

    spread(xs, wb)
    window_scales(xs, band, wcol, mcol, sc)
    finish(correlate(tz, wb, sc), mcol, accs, o_ref)

    z_first.wait_send()
    z_second.wait_send()
    for h in h_copies:
        h.wait_send()
    for s in range(STREAMS):
        for n in range(3):
            x_copy(s, n).wait_send()
        for n in range(4):
            s_copy(s, n).wait_send()


def per_device(waveform, templates, station_index, channel_mask):
    w = jnp.transpose(waveform, (1, 0, 2))
    t = jnp.transpose(templates, (1, 2, 0, 3)).reshape(GROUPS, MEMBERS, TPL)
    mask = jnp.transpose(channel_mask, (2, 0, 1))
    vmem, smem = pl.BlockSpec(memory_space=pltpu.VMEM), pl.BlockSpec(memory_space=pltpu.SMEM)
    dma = pltpu.SemaphoreType.DMA
    return pl.pallas_call(
        kernel,
        out_shape=jax.ShapeDtypeStruct((MEMBERS, TIME), f32),
        in_specs=[vmem, vmem, smem, smem],
        out_specs=vmem,
        scratch_shapes=[
            pltpu.VMEM((16, ROWS, TIME), bf16),
            pltpu.VMEM((16, ROWS, TIME), bf16),
            pltpu.VMEM((ROWS, TIME), bf16),
            pltpu.VMEM((GROUPS, LANES, TIME), bf16),
            pltpu.VMEM((TRACES, LANES), i32),
            pltpu.VMEM((TRACES, LANES), f32),
            pltpu.VMEM((TRACES, LANES), f32),
            pltpu.VMEM((TRACES, 2 * TIME), f32),
            pltpu.VMEM((TRACES * 40, LANES), f32),
            pltpu.VMEM((TRACES * 24, LANES), f32),
            pltpu.VMEM((96, LANES), f32),
            dma((STREAMS, 3)),
            dma((STREAMS, 3)),
            dma((STREAMS, 4)),
            dma((STREAMS, 4)),
            dma((2,)),
            dma((2,)),
            dma((2,)),
            dma((2,)),
        ],
        compiler_params=pltpu.CompilerParams(
            collective_id=0, has_side_effects=True, vmem_limit_bytes=40 * 2**20
        ),
    )(w, t, station_index, mask)


def solution(mesh):
    return jax.shard_map(
        per_device,
        mesh=mesh,
        in_specs=(
            P("blk", None, "tm"),
            P("blk", None, None, None),
            P("blk", None),
            P("blk", None, None),
        ),
        out_specs=P("blk", "tm"),
        check_vma=False,
    )
```

time: 607 us -> 57.3 us (0.09)
  the two profiles are of different devices: /device:TPU:24 before, /device:TPU:1 now
where the time goes in v1:
time: 57.3 us; the launch traced here: 57.1 us
  Pallas kernels  53.3 us (93%)
  local copies, waits for them, and re-layouts  3.8 us (7%)
    pallas_call x1, Pallas kernels, per_device(): pl.pallas_call(kernel, out_shape=jax.ShapeDtypeStruct((MEMBERS, TIME), f3...  53.3 us
    unnamed x9, local copies, waits for them, and re-layouts  3.8 us

profile of v1, /device:TPU:1, one launch (start us, length us, event | category | flops | bytes accessed | tf_op | source)
XLA Modules:
  0.0 57.1 jit_solution(1673699360855317947)
XLA Ops:
  0.0 0.0 copy-start.3
  0.0 0.7 %copy-done.3 = s32[4,12]{1,0:T(4,128)S(1)} copy-done((s32[4,12]{1,0:T(4,128)S(1)}, s32[4,12]{1,0:T(4,128)}, u32[]{:S(2)}) %copy-start.3) | copy-done | bytes 216
  0.7 0.0 copy-start
  0.7 0.9 %copy-done = bf16[4,12,3,600]{3,0,2,1:T(4,128)(2,1)S(1)} copy-done((bf16[4,12,3,600]{3,0,2,1:T(4,128)(2,1)S(1)}, bf16[4,12,3,600]{3,0,2,1:T(4,128)(2,1)}, u32[]{:S(2)}) %copy-start) | copy-done | bytes 172824
  1.6 0.0 copy-start.1
  1.6 0.9 %copy-done.1 = bf16[25,3,640]{2,0,1:T(8,128)(2,1)S(1)} copy-done((bf16[25,3,640]{2,0,1:T(8,128)(2,1)S(1)}, bf16[25,3,640]{2,0,1:T(8,128)(2,1)}, u32[]{:S(2)}) %copy-start.1) | copy-done | bytes 96024
  2.5 0.0 copy-start.2
  2.5 0.7 %copy-done.2 = s32[4,12,3]{1,0,2:T(4,128)S(1)} copy-done((s32[4,12,3]{1,0,2:T(4,128)S(1)}, s32[4,12,3]{1,0,2:T(4,128)}, u32[]{:S(2)}) %copy-start.2) | copy-done | bytes 600
  3.2 53.3 %shard_map.46 = f32[4,640]{1,0:T(4,128)S(1)} custom-call(bf16[3,25,640]{2,1,0:T(8,128)(2,1)S(1)} %bitcast.6, bf16[36,4,600]{2,1,0:T(4,128)(2,1)S(1)} %bitcast.5, s32[4,12]{1,0:T(4,128)S(1)} %copy-done.3, s32[3,4,12]{2,1,0:T(4,128)S(1)} %bitcast.7), custom_call_target="tpu_custom_call" | custom-call | tf_op jit(solution)/shard_map/pallas_call | solution.py:283
  56.5 0.6 %copy.6 = f32[4,640]{1,0:T(4,128)} copy(f32[4,640]{1,0:T(4,128)S(1)} %shard_map.46) | data formatting | bytes 20480
Async XLA Ops:
  0.0 0.7 %copy-start.3 = (s32[4,12]{1,0:T(4,128)S(1)}, s32[4,12]{1,0:T(4,128)}, u32[]{:S(2)}) copy-start(s32[4,12]{1,0:T(4,128)} %idx_ref.1) | copy-start | bytes 580
  0.7 0.9 %copy-start = (bf16[4,12,3,600]{3,0,2,1:T(4,128)(2,1)S(1)}, bf16[4,12,3,600]{3,0,2,1:T(4,128)(2,1)}, u32[]{:S(2)}) copy-start(bf16[4,12,3,600]{3,0,2,1:T(4,128)(2,1)} %param.5) | copy-start | bytes 518404
  1.6 0.9 %copy-start.1 = (bf16[25,3,640]{2,0,1:T(8,128)(2,1)S(1)}, bf16[25,3,640]{2,0,1:T(8,128)(2,1)}, u32[]{:S(2)}) copy-start(bf16[25,3,640]{2,0,1:T(8,128)(2,1)} %param.4) | copy-start | bytes 288004
  2.5 0.7 %copy-start.2 = (s32[4,12,3]{1,0,2:T(4,128)S(1)}, s32[4,12,3]{1,0,2:T(4,128)}, u32[]{:S(2)}) copy-start(s32[4,12,3]{1,0,2:T(4,128)} %param.7) | copy-start | bytes 1732

commit v2 on v1

v2 whole, which is shorter than its diff:
```python
import jax
import jax.numpy as jnp
from jax import lax
from jax.experimental import pallas as pl
from jax.experimental.pallas import tpu as pltpu
from jax.sharding import PartitionSpec as P

bf16, f32, i32 = jnp.bfloat16, jnp.float32, jnp.int32
MESH = pl.DeviceIdType.MESH
NT = (((1,), (1,)), ((), ()))

TPL = 600
TIME = 640
PER = 25
ROWS = 80
SUB = 32
LANES = 128
GROUPS = 36
MEMBERS = 4
TRACES = GROUPS * MEMBERS
HALF = 8 * ROWS
SLOTS = 8
QUARTER = GROUPS // 4


def build_toeplitz(t_ref, tz, wcol, base):
    def body(g, carry):
        tt = t_ref[pl.ds(2 * g, 2)].astype(f32).reshape(8, TPL)
        norm = lax.rsqrt(jnp.sum(tt * tt, axis=1, keepdims=True) + 1e-6)
        wcol[pl.ds(pl.multiple_of(base + 8 * g, 8), 8), :] = jnp.broadcast_to(norm, (8, LANES))
        padded = jnp.concatenate([tt, jnp.zeros((8, TIME - TPL), f32)], axis=1)
        for i in range(8):
            rows = jnp.broadcast_to(padded[i : i + 1], (SUB, TIME))
            tz[2 * g + i // 4, pl.ds(SUB * (i % 4), SUB), :] = pltpu.roll(
                rows, 0, 1, stride=1, stride_axis=0
            ).astype(bf16)
        return carry

    lax.fori_loop(0, GROUPS // 2, body, 0)


def number_rows(idx_ref, mask_ref, zh, mine, theirs, mcol):
    def body(g, carry):
        row0 = pl.multiple_of(8 * g, 8)
        for i in range(8):
            jc = 2 * g + i // 4
            k = i % 4
            j = jc // 3
            c = jc - 3 * j
            station = idx_ref[k, j]
            used = mask_ref[c, k, j]
            owner = station // PER
            half = owner // 8
            row = ((owner - 8 * half) * ROWS + c * PER + (station - PER * owner) + 1) * used
            here = half * zh + (1 - half) * (1 - zh)
            mine[pl.ds(row0 + i, 1), :] = jnp.full((1, LANES), (row * here).astype(f32), f32)
            theirs[pl.ds(row0 + i, 1), :] = jnp.full((1, LANES), (row * (1 - here)).astype(f32), f32)
            mcol[pl.ds(row0 + i, 1), :] = jnp.full((1, LANES), used.astype(f32), f32)
        return carry

    lax.fori_loop(0, GROUPS // 2, body, 0)


def band_matrix():
    u = lax.broadcasted_iota(i32, (768, LANES), 0)
    b = lax.broadcasted_iota(i32, (768, LANES), 1)
    d = u - b
    return jnp.where((d >= 0) & (d < TPL), 1.0, 0.0).astype(bf16)


def choose(rows, ids, base):
    number = lax.broadcasted_iota(i32, (TRACES, HALF), 1).astype(f32) + 1.0
    ids[pl.ds(base, TRACES), :] = jnp.where(jnp.broadcast_to(rows, (TRACES, HALF)) == number, 1.0, 0.0).astype(bf16)


def pick(ids, store, first, count):
    blocks = [store[:, first + i].reshape(HALF, LANES) for i in range(count)]
    return jnp.dot(ids, jnp.concatenate(blocks, axis=1), preferred_element_type=f32)


def spread(xs, wb, base):
    full = xs[pl.ds(base, TRACES), :]
    for a in range(4):
        moved = full if a == 0 else pltpu.roll(full, 2 * TIME - SUB * a, 1)
        for m in range(10):
            wb[pl.ds(40 * base + 4 * m + a, TRACES, stride=40), :] = moved[:, LANES * m : LANES * (m + 1)]


def window_scales(xs, band, sc, base):
    high, low = [], []
    for m in range(10):
        part = xs[pl.ds(base, TRACES), LANES * m : LANES * (m + 1)]
        square = part * part
        top = square.astype(bf16)
        high.append(top)
        low.append((square - top.astype(f32)).astype(bf16))
    lane = lax.broadcasted_iota(i32, (TRACES, LANES), 1) // SUB
    member = lax.rem(lax.broadcasted_iota(i32, (TRACES, LANES), 0), MEMBERS)
    for a in range(5):
        energy = jnp.dot(jnp.concatenate(high[a : a + 6], axis=1), band, preferred_element_type=f32)
        energy += jnp.dot(jnp.concatenate(low[a : a + 6], axis=1), band, preferred_element_type=f32)
        scale = lax.rsqrt(jnp.maximum(energy, 0.25 * TPL))
        turned = [scale] + [pltpu.roll(scale, SUB * d, 1) for d in range(1, 4)]
        for a2 in range(4):
            v = jnp.zeros((TRACES, LANES), f32)
            for k in range(MEMBERS):
                v = jnp.where((lane == k) & (member == k), turned[(k - a2) % 4], v)
            sc[pl.ds(24 * base + 4 * a + a2, TRACES, stride=24), :] = v


def correlate(tz, wb, sc, wcol, base, unroll=6):
    def body(g, acc):
        for q in range(unroll):
            jc = g * unroll + q
            parts, gains = [], []
            for k in range(MEMBERS):
                trace = base + jc * MEMBERS + k
                row = pl.multiple_of(trace * 40, 8)
                parts.append(jnp.concatenate([wb[pl.ds(row + 4 * p, 24), :] for p in range(5)], axis=1))
                gains.append(jnp.broadcast_to(wcol[pl.ds(trace, 1), :], (24, LANES)))
            windows = jnp.concatenate(parts, axis=0).astype(bf16)
            c = lax.dot_general(windows, tz[jc], NT, preferred_element_type=f32)
            scale = sc[pl.ds(pl.multiple_of((base + jc * MEMBERS) * 24, 8), 96), :]
            acc = acc + c * (scale * jnp.concatenate(gains, axis=0))
        return acc

    acc = lax.fori_loop(0, GROUPS // unroll, body, jnp.zeros((96, LANES), f32))
    return (acc[0:24] + acc[24:48]) + (acc[48:72] + acc[72:96])


def finish(sums, mcol, o_ref):
    counts = jnp.sum(mcol[...].reshape(GROUPS, MEMBERS, LANES), axis=0)
    factor = jnp.sqrt(TPL / counts)
    lane = lax.broadcasted_iota(i32, (8, LANES), 1) // SUB
    quads = [sums[pl.ds(q, 5, stride=4), :] for q in range(4)]
    quads = [jnp.concatenate([rows, jnp.zeros((3, LANES), f32)], axis=0) for rows in quads]
    for k in range(MEMBERS):
        out = jnp.zeros((8, LANES), f32)
        for q in range(4):
            rows = quads[q] if q == k else pltpu.roll(quads[q], (SUB * (q - k)) % LANES, 1)
            out = jnp.where(lane == q, rows, out)
        for m in range(5):
            o_ref[k : k + 1, LANES * m : LANES * (m + 1)] = out[m : m + 1, :] * factor[k : k + 1, :]


def kernel(
    w_hbm, t_hbm, idx_hbm, mask_hbm, o_ref,
    w_ref, t_ref, idx_ref, mask_ref, t_far, n_out, n_in, gm, gh, ids, tz, tz_far, mine, theirs, wcol, mcol,
    xs, wb, sc, r_out, r_in, sums,
    in_sem, x_send, x_recv, s_send, s_recv, h_send, h_recv, t_send, t_recv, y_send, y_recv, n_send, n_recv, r_send, r_recv,
):
    blk, tm = lax.axis_index("blk"), lax.axis_index("tm")
    zh, x, core = blk // 8, lax.rem(blk // 2, 4), lax.rem(blk, 2)
    zl, y = tm // 4, lax.rem(tm, 4)

    def at(place, c):
        return lax.rem(place + 4, 4) * 2 + c

    loads = [
        pltpu.make_async_copy(src, dst, in_sem.at[i])
        for i, (src, dst) in enumerate(
            ((w_hbm, w_ref), (idx_hbm, idx_ref), (mask_hbm, mask_ref), (t_hbm, t_ref))
        )
    ]
    for load in loads:
        load.start()

    other = (1 - zh) * 8 + at(x, core)
    partner = (other, tm)
    mirror = (other, (7 - zl) * 4 + y)
    sibling = (zh * 8 + at(x, 1 - core), tm)
    across = [(zh * 8 + at(x + d, core), tm) for d in (1, -1, 2)]
    column = [(blk, zl * 4 + lax.rem(y + d + 4, 4)) for d in (1, -1, 2)]
    earlier, later = (blk, lax.rem(tm + 31, 32)), (blk, lax.rem(tm + 1, 32))
    has_earlier, has_later = tm > 0, tm < 31

    barrier = pltpu.get_barrier_semaphore()
    friends = (mirror, partner, *across, *column, sibling)
    for friend in friends:
        pl.semaphore_signal(barrier, inc=1, device_id=friend, device_id_type=MESH)

    @pl.when(has_earlier)
    def _():
        pl.semaphore_signal(barrier, inc=1, device_id=earlier, device_id_type=MESH)

    @pl.when(has_later)
    def _():
        pl.semaphore_signal(barrier, inc=1, device_id=later, device_id_type=MESH)

    loads[0].wait()
    own = w_ref[...].astype(f32)
    packed = jnp.concatenate([own[0], own[1], own[2], jnp.zeros((ROWS - 3 * PER, TIME), f32)], axis=0)
    slot = at(x, core)
    for m in range(5):
        gm[slot, m] = packed[:, LANES * m : LANES * (m + 1)].astype(bf16)
    pl.semaphore_wait(barrier, len(friends) + has_earlier.astype(i32) + has_later.astype(i32))

    def copy(src, dst, send, recv, to):
        return pltpu.make_async_remote_copy(
            src_ref=src, dst_ref=dst, send_sem=send, recv_sem=recv, device_id=to, device_id_type=MESH
        )

    store = (gm, gh)

    def x_copy(s, n):
        block = store[s].at[slot]
        return copy(block, block, x_send.at[s, n], x_recv.at[s, n], across[n])

    def x_wait(s, n):
        block = store[s].at[at(x + (-1, 1, 2)[n], core)]
        copy(block, block, x_send.at[s, n], x_recv.at[s, n], across[n]).wait_recv()

    def s_copy(s, n):
        block = store[s].at[at(x + (0, -1, 1, 2)[n], core)]
        return copy(block, block, s_send.at[s, n], s_recv.at[s, n], sibling)

    def s_wait(s):
        for n in range(4):
            block = store[s].at[at(x + (0, -1, 1, 2)[n], 1 - core)]
            copy(block, block, s_send.at[s, n], s_recv.at[s, n], sibling).wait_recv()

    h_copy = copy(gm.at[slot], gh.at[slot], h_send, h_recv, earlier)

    def quarter(ref, part):
        return ref.at[pl.ds(QUARTER * lax.rem(part + 4, 4), QUARTER)]

    t_copy = copy(quarter(t_hbm, y), quarter(t_far, y), t_send, t_recv, mirror)

    def y_copy(n):
        block = quarter(t_far, y)
        return copy(block, block, y_send.at[n], y_recv.at[n], column[n])

    def y_wait(n):
        block = quarter(t_far, y + (-1, 1, 2)[n])
        copy(block, block, y_send.at[n], y_recv.at[n], column[n]).wait_recv()

    n_copy = copy(n_out, n_in, n_send, n_recv, mirror)
    r_copy = copy(r_out, r_in, r_send, r_recv, partner)

    def fan(s):
        for n in range(3):
            x_copy(s, n).start()
        s_copy(s, 0).start()

    def hand_over(s):
        for n in range(3):
            x_wait(s, n)
            s_copy(s, 1 + n).start()

    t_copy.start()

    @pl.when(has_earlier)
    def _():
        h_copy.start()

    fan(0)
    loads[1].wait()
    loads[2].wait()
    number_rows(idx_ref, mask_ref, zh, mine, theirs, mcol)
    flat = jnp.transpose(theirs[...])[0:8, :]
    sixteens = jnp.floor(flat * (1.0 / 16.0))
    n_out[...] = jnp.concatenate([sixteens, flat - 16.0 * sixteens], axis=0).astype(bf16)
    n_copy.start()
    loads[3].wait()
    choose(mine[0:TRACES, 0:1], ids, 0)

    @pl.when(has_later)
    def _():
        h_copy.wait_recv()

    @pl.when(jnp.logical_not(has_later))
    def _():
        for m in range(5):
            gh[slot, m] = jnp.zeros((ROWS, LANES), bf16)

    fan(1)
    hand_over(0)
    build_toeplitz(t_ref, tz, wcol, 0)
    n_copy.wait_recv()
    got = n_in[...].astype(f32)
    choose(jnp.transpose(got[0:8] * 16.0 + got[8:16])[0:TRACES, 0:1], ids, TRACES)
    t_copy.wait_recv()
    for n in range(3):
        y_copy(n).start()
    s_wait(0)
    xs[:, :TIME] = pick(ids[...], gm, 0, 5)
    hand_over(1)
    s_wait(1)
    xs[:, TIME:] = pick(ids[...], gh, 0, 5)
    band = band_matrix()
    for base in (TRACES, 0):
        spread(xs, wb, base)
        window_scales(xs, band, sc, base)
    for n in range(3):
        y_wait(n)
    build_toeplitz(t_far, tz_far, wcol, TRACES)
    r_out[...] = correlate(tz_far, wb, sc, wcol, TRACES)
    r_copy.start()
    total = correlate(tz, wb, sc, wcol, 0)
    r_copy.wait_recv()
    sums[...] = total + r_in[...]
    finish(sums, mcol, o_ref)

    for n in range(3):
        y_copy(n).wait_send()
        for s in range(2):
            x_copy(s, n).wait_send()
    for n in range(4):
        for s in range(2):
            s_copy(s, n).wait_send()
    for sent in (t_copy, n_copy, r_copy):
        sent.wait_send()

    @pl.when(has_earlier)
    def _():
        h_copy.wait_send()


def per_device(waveform, templates, station_index, channel_mask):
    w = jnp.transpose(waveform, (1, 0, 2))
    t = jnp.transpose(templates, (1, 2, 0, 3)).reshape(GROUPS, MEMBERS, TPL)
    mask = jnp.transpose(channel_mask, (2, 0, 1))
    anywhere = pl.BlockSpec(memory_space=pl.ANY)
    dma = pltpu.SemaphoreType.DMA
    return pl.pallas_call(
        kernel,
        out_shape=jax.ShapeDtypeStruct((MEMBERS, TIME), f32),
        in_specs=[anywhere] * 4,
        out_specs=pl.BlockSpec(memory_space=pltpu.VMEM),
        scratch_shapes=[
            pltpu.VMEM(w.shape, bf16),
            pltpu.VMEM(t.shape, bf16),
            pltpu.SMEM(station_index.shape, i32),
            pltpu.SMEM(mask.shape, i32),
            pltpu.VMEM(t.shape, bf16),
            pltpu.VMEM((16, 256), bf16),
            pltpu.VMEM((16, 256), bf16),
            pltpu.VMEM((SLOTS, 5, ROWS, LANES), bf16),
            pltpu.VMEM((SLOTS, 5, ROWS, LANES), bf16),
            pltpu.VMEM((2 * TRACES, HALF), bf16),
            pltpu.VMEM((GROUPS, LANES, TIME), bf16),
            pltpu.VMEM((GROUPS, LANES, TIME), bf16),
            pltpu.VMEM((256, LANES), f32),
            pltpu.VMEM((256, LANES), f32),
            pltpu.VMEM((2 * TRACES, LANES), f32),
            pltpu.VMEM((TRACES, LANES), f32),
            pltpu.VMEM((2 * TRACES, 2 * TIME), f32),
            pltpu.VMEM((2 * TRACES * 40, LANES), f32),
            pltpu.VMEM((2 * TRACES * 24, LANES), f32),
            pltpu.VMEM((24, LANES), f32),
            pltpu.VMEM((24, LANES), f32),
            pltpu.VMEM((24, LANES), f32),
            dma((4,)),
            dma((2, 3)),
            dma((2, 3)),
            dma((2, 4)),
            dma((2, 4)),
            dma,
            dma,
            dma,
            dma,
            dma((3,)),
            dma((3,)),
            dma,
            dma,
            dma,
            dma,
        ],
        compiler_params=pltpu.CompilerParams(
            collective_id=0, has_side_effects=True, vmem_limit_bytes=56 * 2**20
        ),
    )(w, t, station_index, mask)


def solution(mesh):
    return jax.shard_map(
        per_device,
        mesh=mesh,
        in_specs=(
            P("blk", None, "tm"),
            P("blk", None, None, None),
            P("blk", None),
            P("blk", None, None),
        ),
        out_specs=P("blk", "tm"),
        check_vma=False,
    )
```

time: 57.3 us -> 46.5 us (0.81)
  the two profiles are of different devices: /device:TPU:1 before, /device:TPU:24 now
where the time goes in v2:
time: 46.5 us; the launch traced here: 45.7 us
  Pallas kernels  44.4 us (95%)
  local copies, waits for them, and re-layouts  1.3 us (3%)
    pallas_call x1, Pallas kernels, per_device(): pl.pallas_call(kernel, out_shape=jax.ShapeDtypeStruct((MEMBERS, TIME), f3...  44.4 us
    unnamed x1, local copies, waits for them, and re-layouts  1.3 us

profile of v2, /device:TPU:24, one launch (start us, length us, event | category | flops | bytes accessed | tf_op | source)
XLA Modules:
  0.0 45.7 jit_solution(9933537389981976104)
XLA Ops:
  0.0 44.4 %shard_map.46 = f32[4,640]{1,0:T(4,128)} custom-call(bf16[3,25,640]{2,1,0:T(8,128)(2,1)} %bitcast.6, bf16[36,4,600]{2,1,0:T(4,128)(2,1)} %bitcast.5, s32[4,12]{1,0:T(4,128)} %idx_hbm.1, s32[3,4,12]{2,1,0:T(4,128)} %bitcast.7), custom_call_target="tpu_custom_call" | custom-call | tf_op jit(solution)/shard_map/pallas_call | solution.py:325
  44.4 1.3 %copy.6 = f32[4,640]{1,0:T(4,128)} copy(f32[4,640]{1,0:T(4,128)} %shard_map.46) | data formatting | bytes 20480

commit v3 on v2

--- a/solution.py
+++ b/solution.py
@@ -23,20 +23,20 @@
 QUARTER = GROUPS // 4
 
 
-def build_toeplitz(t_ref, tz, wcol, base):
+def build_toeplitz(t_ref, tz, wcol, first, count, step=3):
     def body(g, carry):
-        tt = t_ref[pl.ds(2 * g, 2)].astype(f32).reshape(8, TPL)
-        norm = lax.rsqrt(jnp.sum(tt * tt, axis=1, keepdims=True) + 1e-6)
-        wcol[pl.ds(pl.multiple_of(base + 8 * g, 8), 8), :] = jnp.broadcast_to(norm, (8, LANES))
-        padded = jnp.concatenate([tt, jnp.zeros((8, TIME - TPL), f32)], axis=1)
-        for i in range(8):
-            rows = jnp.broadcast_to(padded[i : i + 1], (SUB, TIME))
-            tz[2 * g + i // 4, pl.ds(SUB * (i % 4), SUB), :] = pltpu.roll(
-                rows, 0, 1, stride=1, stride_axis=0
-            ).astype(bf16)
+        group = first + step * g
+        tt = t_ref[pl.ds(group, step)].astype(f32)
+        norm = lax.rsqrt(jnp.sum(tt * tt, axis=2, keepdims=True) + 1e-6)
+        wcol[pl.ds(group, step)] = jnp.broadcast_to(norm, (step, MEMBERS, LANES))
+        padded = jnp.concatenate([tt, jnp.zeros((step, MEMBERS, TIME - TPL), f32)], axis=2)
+        for i in range(step):
+            for k in range(MEMBERS):
+                rows = jnp.broadcast_to(padded[i, k : k + 1], (SUB, TIME))
+                tz[group + i, pl.ds(SUB * k, SUB), :] = pltpu.roll(rows, 0, 1, stride=1, stride_axis=0).astype(bf16)
         return carry
 
-    lax.fori_loop(0, GROUPS // 2, body, 0)
+    lax.fori_loop(0, count // step, body, 0)
 
 
 def number_rows(idx_ref, mask_ref, zh, mine, theirs, mcol):
@@ -108,23 +108,25 @@
             sc[pl.ds(24 * base + 4 * a + a2, TRACES, stride=24), :] = v
 
 
-def correlate(tz, wb, sc, wcol, base, unroll=6):
+def correlate(tz, wb, sc, wcol, base, first, count, acc, unroll=9):
     def body(g, acc):
         for q in range(unroll):
-            jc = g * unroll + q
+            jc = first + g * unroll + q
             parts, gains = [], []
             for k in range(MEMBERS):
-                trace = base + jc * MEMBERS + k
-                row = pl.multiple_of(trace * 40, 8)
+                row = pl.multiple_of((base + jc * MEMBERS + k) * 40, 8)
                 parts.append(jnp.concatenate([wb[pl.ds(row + 4 * p, 24), :] for p in range(5)], axis=1))
-                gains.append(jnp.broadcast_to(wcol[pl.ds(trace, 1), :], (24, LANES)))
+                gains.append(jnp.broadcast_to(wcol[jc, k : k + 1, :], (24, LANES)))
             windows = jnp.concatenate(parts, axis=0).astype(bf16)
             c = lax.dot_general(windows, tz[jc], NT, preferred_element_type=f32)
             scale = sc[pl.ds(pl.multiple_of((base + jc * MEMBERS) * 24, 8), 96), :]
             acc = acc + c * (scale * jnp.concatenate(gains, axis=0))
         return acc
 
-    acc = lax.fori_loop(0, GROUPS // unroll, body, jnp.zeros((96, LANES), f32))
+    return lax.fori_loop(0, count // unroll, body, acc)
+
+
+def fold(acc):
     return (acc[0:24] + acc[24:48]) + (acc[48:72] + acc[72:96])
 
 
@@ -145,7 +147,7 @@
 
 def kernel(
     w_hbm, t_hbm, idx_hbm, mask_hbm, o_ref,
-    w_ref, t_ref, idx_ref, mask_ref, t_far, n_out, n_in, gm, gh, ids, tz, tz_far, mine, theirs, wcol, mcol,
+    w_ref, t_ref, idx_ref, mask_ref, t_far, n_out, n_in, gm, gh, ids, tz, tz_far, mine, theirs, wcol, wcol_far, mcol,
     xs, wb, sc, r_out, r_in, sums,
     in_sem, x_send, x_recv, s_send, s_recv, h_send, h_recv, t_send, t_recv, y_send, y_recv, n_send, n_recv, r_send, r_recv,
 ):
@@ -193,6 +195,8 @@
     slot = at(x, core)
     for m in range(5):
         gm[slot, m] = packed[:, LANES * m : LANES * (m + 1)].astype(bf16)
+    loads[3].wait()
+    build_toeplitz(t_ref, tz, wcol, 0, GROUPS)
     pl.semaphore_wait(barrier, len(friends) + has_earlier.astype(i32) + has_later.astype(i32))
 
     def copy(src, dst, send, recv, to):
@@ -219,7 +223,26 @@
             block = store[s].at[at(x + (0, -1, 1, 2)[n], 1 - core)]
             copy(block, block, s_send.at[s, n], s_recv.at[s, n], sibling).wait_recv()
 
-    h_copy = copy(gm.at[slot], gh.at[slot], h_send, h_recv, earlier)
+    facing = at(x + 2, core)
+    h_copies = [
+        copy(gm.at[place], gh.at[place], h_send.at[n], h_recv.at[n], earlier) for n, place in enumerate((slot, facing))
+    ]
+
+    def h_start(n):
+        @pl.when(has_earlier)
+        def _():
+            h_copies[n].start()
+
+    def h_wait(n):
+        @pl.when(has_later)
+        def _():
+            h_copies[n].wait_recv()
+
+        @pl.when(jnp.logical_not(has_later))
+        def _():
+            for m in range(5):
+                gh[(slot, facing)[n], m] = jnp.zeros((ROWS, LANES), bf16)
+
 
     def quarter(ref, part):
         return ref.at[pl.ds(QUARTER * lax.rem(part + 4, 4), QUARTER)]
@@ -237,23 +260,11 @@
     n_copy = copy(n_out, n_in, n_send, n_recv, mirror)
     r_copy = copy(r_out, r_in, r_send, r_recv, partner)
 
-    def fan(s):
-        for n in range(3):
-            x_copy(s, n).start()
-        s_copy(s, 0).start()
-
-    def hand_over(s):
-        for n in range(3):
-            x_wait(s, n)
-            s_copy(s, 1 + n).start()
-
     t_copy.start()
-
-    @pl.when(has_earlier)
-    def _():
-        h_copy.start()
-
-    fan(0)
+    h_start(0)
+    for n in range(3):
+        x_copy(0, n).start()
+    s_copy(0, 0).start()
     loads[1].wait()
     loads[2].wait()
     number_rows(idx_ref, mask_ref, zh, mine, theirs, mcol)
@@ -261,50 +272,55 @@
     sixteens = jnp.floor(flat * (1.0 / 16.0))
     n_out[...] = jnp.concatenate([sixteens, flat - 16.0 * sixteens], axis=0).astype(bf16)
     n_copy.start()
-    loads[3].wait()
     choose(mine[0:TRACES, 0:1], ids, 0)
-
-    @pl.when(has_later)
-    def _():
-        h_copy.wait_recv()
-
-    @pl.when(jnp.logical_not(has_later))
-    def _():
-        for m in range(5):
-            gh[slot, m] = jnp.zeros((ROWS, LANES), bf16)
-
-    fan(1)
-    hand_over(0)
-    build_toeplitz(t_ref, tz, wcol, 0)
+    h_wait(0)
+    for n in range(2):
+        x_copy(1, n).start()
+    s_copy(1, 0).start()
+    x_wait(0, 2)
+    h_start(1)
+    s_copy(0, 3).start()
+    t_copy.wait_recv()
+    for n in range(3):
+        y_copy(n).start()
+    for n in range(2):
+        x_wait(0, n)
+        s_copy(0, 1 + n).start()
+    build_toeplitz(t_far, tz_far, wcol_far, QUARTER * y, QUARTER)
     n_copy.wait_recv()
     got = n_in[...].astype(f32)
     choose(jnp.transpose(got[0:8] * 16.0 + got[8:16])[0:TRACES, 0:1], ids, TRACES)
-    t_copy.wait_recv()
-    for n in range(3):
-        y_copy(n).start()
+    h_wait(1)
+    s_copy(1, 3).start()
+    for n in range(2):
+        x_wait(1, n)
+        s_copy(1, 1 + n).start()
     s_wait(0)
     xs[:, :TIME] = pick(ids[...], gm, 0, 5)
-    hand_over(1)
+    band = band_matrix()
+    for n in range(3):
+        y_wait(n)
+        build_toeplitz(t_far, tz_far, wcol_far, QUARTER * lax.rem(y + (3, 1, 2)[n], 4), QUARTER)
     s_wait(1)
     xs[:, TIME:] = pick(ids[...], gh, 0, 5)
-    band = band_matrix()
-    for base in (TRACES, 0):
-        spread(xs, wb, base)
-        window_scales(xs, band, sc, base)
-    for n in range(3):
-        y_wait(n)
-    build_toeplitz(t_far, tz_far, wcol, TRACES)
-    r_out[...] = correlate(tz_far, wb, sc, wcol, TRACES)
+    spread(xs, wb, TRACES)
+    window_scales(xs, band, sc, TRACES)
+    acc = jnp.zeros((96, LANES), f32)
+    acc = correlate(tz_far, wb, sc, wcol_far, TRACES, 0, GROUPS, acc, 12)
+    r_out[...] = fold(acc)
     r_copy.start()
-    total = correlate(tz, wb, sc, wcol, 0)
+    spread(xs, wb, 0)
+    window_scales(xs, band, sc, 0)
+    total = fold(correlate(tz, wb, sc, wcol, 0, 0, GROUPS, jnp.zeros((96, LANES), f32), 12))
     r_copy.wait_recv()
     sums[...] = total + r_in[...]
     finish(sums, mcol, o_ref)
 
     for n in range(3):
         y_copy(n).wait_send()
-        for s in range(2):
-            x_copy(s, n).wait_send()
+        x_copy(0, n).wait_send()
+    for n in range(2):
+        x_copy(1, n).wait_send()
     for n in range(4):
         for s in range(2):
             s_copy(s, n).wait_send()
@@ -313,7 +329,8 @@
 
     @pl.when(has_earlier)
     def _():
-        h_copy.wait_send()
+        for h in h_copies:
+            h.wait_send()
 
 
 def per_device(waveform, templates, station_index, channel_mask):
@@ -342,7 +359,8 @@
             pltpu.VMEM((GROUPS, LANES, TIME), bf16),
             pltpu.VMEM((256, LANES), f32),
             pltpu.VMEM((256, LANES), f32),
-            pltpu.VMEM((2 * TRACES, LANES), f32),
+            pltpu.VMEM((GROUPS, MEMBERS, LANES), f32),
+            pltpu.VMEM((GROUPS, MEMBERS, LANES), f32),
             pltpu.VMEM((TRACES, LANES), f32),
             pltpu.VMEM((2 * TRACES, 2 * TIME), f32),
             pltpu.VMEM((2 * TRACES * 40, LANES), f32),
@@ -355,8 +373,8 @@
             dma((2, 3)),
             dma((2, 4)),
             dma((2, 4)),
-            dma,
-            dma,
+            dma((2,)),
+            dma((2,)),
             dma,
             dma,
             dma((3,)),

time: 46.5 us -> 42.9 us (0.923)
  the two profiles are of different devices: /device:TPU:24 before, /device:TPU:8 now
where the time goes in v3:
time: 42.9 us; the launch traced here: 42.7 us
  Pallas kernels  41.4 us (97%)
  local copies, waits for them, and re-layouts  1.3 us (3%)
    pallas_call x1, Pallas kernels, per_device(): pl.pallas_call(kernel, out_shape=jax.ShapeDtypeStruct((MEMBERS, TIME), f3...  41.4 us
    unnamed x1, local copies, waits for them, and re-layouts  1.3 us

profile of v3, /device:TPU:8, one launch (start us, length us, event | category | flops | bytes accessed | tf_op | source)
XLA Modules:
  0.0 42.7 jit_solution(2367330972842660541)
XLA Ops:
  0.0 41.4 %shard_map.46 = f32[4,640]{1,0:T(4,128)} custom-call(bf16[3,25,640]{2,1,0:T(8,128)(2,1)} %bitcast.6, bf16[36,4,600]{2,1,0:T(4,128)(2,1)} %bitcast.5, s32[4,12]{1,0:T(4,128)} %idx_hbm.1, s32[3,4,12]{2,1,0:T(4,128)} %bitcast.7), custom_call_target="tpu_custom_call" | custom-call | tf_op jit(solution)/shard_map/pallas_call | solution.py:342
  41.4 1.3 %copy.6 = f32[4,640]{1,0:T(4,128)} copy(f32[4,640]{1,0:T(4,128)} %shard_map.46) | data formatting | bytes 20480

commit v4 on v3

--- a/solution.py
+++ b/solution.py
@@ -177,7 +177,7 @@
     has_earlier, has_later = tm > 0, tm < 31
 
     barrier = pltpu.get_barrier_semaphore()
-    friends = (mirror, partner, *across, *column, sibling)
+    friends = (*across, *column, sibling, mirror, partner)
     for friend in friends:
         pl.semaphore_signal(barrier, inc=1, device_id=friend, device_id_type=MESH)
 
@@ -195,8 +195,6 @@
     slot = at(x, core)
     for m in range(5):
         gm[slot, m] = packed[:, LANES * m : LANES * (m + 1)].astype(bf16)
-    loads[3].wait()
-    build_toeplitz(t_ref, tz, wcol, 0, GROUPS)
     pl.semaphore_wait(barrier, len(friends) + has_earlier.astype(i32) + has_later.astype(i32))
 
     def copy(src, dst, send, recv, to):
@@ -262,7 +260,7 @@
 
     t_copy.start()
     h_start(0)
-    for n in range(3):
+    for n in (2, 0, 1):
         x_copy(0, n).start()
     s_copy(0, 0).start()
     loads[1].wait()
@@ -273,6 +271,8 @@
     n_out[...] = jnp.concatenate([sixteens, flat - 16.0 * sixteens], axis=0).astype(bf16)
     n_copy.start()
     choose(mine[0:TRACES, 0:1], ids, 0)
+    loads[3].wait()
+    build_toeplitz(t_ref, tz, wcol, 0, GROUPS)
     h_wait(0)
     for n in range(2):
         x_copy(1, n).start()
@@ -302,13 +302,14 @@
         y_wait(n)
         build_toeplitz(t_far, tz_far, wcol_far, QUARTER * lax.rem(y + (3, 1, 2)[n], 4), QUARTER)
     s_wait(1)
-    xs[:, TIME:] = pick(ids[...], gh, 0, 5)
+    xs[pl.ds(TRACES, TRACES), TIME:] = pick(ids[pl.ds(TRACES, TRACES), :], gh, 0, 5)
     spread(xs, wb, TRACES)
     window_scales(xs, band, sc, TRACES)
     acc = jnp.zeros((96, LANES), f32)
-    acc = correlate(tz_far, wb, sc, wcol_far, TRACES, 0, GROUPS, acc, 12)
+    acc = correlate(tz_far, wb, sc, wcol_far, TRACES, 0, GROUPS, acc, 36)
     r_out[...] = fold(acc)
     r_copy.start()
+    xs[pl.ds(0, TRACES), TIME:] = pick(ids[pl.ds(0, TRACES), :], gh, 0, 5)
     spread(xs, wb, 0)
     window_scales(xs, band, sc, 0)
     total = fold(correlate(tz, wb, sc, wcol, 0, 0, GROUPS, jnp.zeros((96, LANES), f32), 12))

time: 42.9 us -> 40.9 us (0.953)
  the two profiles are of different devices: /device:TPU:8 before, /device:TPU:24 now
where the time goes in v4:
time: 40.9 us; the launch traced here: 40.7 us
  Pallas kernels  39.4 us (96%)
  local copies, waits for them, and re-layouts  1.3 us (3%)
    pallas_call x1, Pallas kernels, per_device(): pl.pallas_call(kernel, out_shape=jax.ShapeDtypeStruct((MEMBERS, TIME), f3...  39.4 us
    unnamed x1, local copies, waits for them, and re-layouts  1.3 us

profile of v4, /device:TPU:24, one launch (start us, length us, event | category | flops | bytes accessed | tf_op | source)
XLA Modules:
  0.0 40.7 jit_solution(8085826762880883825)
XLA Ops:
  0.0 39.4 %shard_map.46 = f32[4,640]{1,0:T(4,128)} custom-call(bf16[3,25,640]{2,1,0:T(8,128)(2,1)} %bitcast.6, bf16[36,4,600]{2,1,0:T(4,128)(2,1)} %bitcast.5, s32[4,12]{1,0:T(4,128)} %idx_hbm.1, s32[3,4,12]{2,1,0:T(4,128)} %bitcast.7), custom_call_target="tpu_custom_call" | custom-call | tf_op jit(solution)/shard_map/pallas_call | solution.py:343
  39.4 1.3 %copy.6 = f32[4,640]{1,0:T(4,128)} copy(f32[4,640]{1,0:T(4,128)} %shard_map.46) | data formatting | bytes 20480

commit v5 on v4

--- a/solution.py
+++ b/solution.py
@@ -21,6 +21,7 @@
 HALF = 8 * ROWS
 SLOTS = 8
 QUARTER = GROUPS // 4
+PIECE = QUARTER // 3
 
 
 def build_toeplitz(t_ref, tz, wcol, first, count, step=3):
@@ -149,7 +150,7 @@
     w_hbm, t_hbm, idx_hbm, mask_hbm, o_ref,
     w_ref, t_ref, idx_ref, mask_ref, t_far, n_out, n_in, gm, gh, ids, tz, tz_far, mine, theirs, wcol, wcol_far, mcol,
     xs, wb, sc, r_out, r_in, sums,
-    in_sem, x_send, x_recv, s_send, s_recv, h_send, h_recv, t_send, t_recv, y_send, y_recv, n_send, n_recv, r_send, r_recv,
+    in_sem, x_send, x_recv, s_send, s_recv, h_send, h_recv, t_send, t_recv, y_send, y_recv, n_send, n_recv, r_send, r_recv, meet,
 ):
     blk, tm = lax.axis_index("blk"), lax.axis_index("tm")
     zh, x, core = blk // 8, lax.rem(blk // 2, 4), lax.rem(blk, 2)
@@ -177,9 +178,15 @@
     has_earlier, has_later = tm > 0, tm < 31
 
     barrier = pltpu.get_barrier_semaphore()
-    friends = (*across, *column, sibling, mirror, partner)
+    friends = (*across, *column, sibling, mirror)
     for friend in friends:
         pl.semaphore_signal(barrier, inc=1, device_id=friend, device_id_type=MESH)
+
+    first_half = zh == 0
+
+    @pl.when(first_half)
+    def _():
+        pl.semaphore_signal(barrier, inc=1, device_id=partner, device_id_type=MESH)
 
     @pl.when(has_earlier)
     def _():
@@ -195,7 +202,11 @@
     slot = at(x, core)
     for m in range(5):
         gm[slot, m] = packed[:, LANES * m : LANES * (m + 1)].astype(bf16)
-    pl.semaphore_wait(barrier, len(friends) + has_earlier.astype(i32) + has_later.astype(i32))
+    pl.semaphore_wait(barrier, len(friends) + zh + has_earlier.astype(i32) + has_later.astype(i32))
+
+    @pl.when(jnp.logical_not(first_half))
+    def _():
+        pl.semaphore_signal(meet, inc=1, device_id=partner, device_id_type=MESH)
 
     def copy(src, dst, send, recv, to):
         return pltpu.make_async_remote_copy(
@@ -242,23 +253,33 @@
                 gh[(slot, facing)[n], m] = jnp.zeros((ROWS, LANES), bf16)
 
 
-    def quarter(ref, part):
-        return ref.at[pl.ds(QUARTER * lax.rem(part + 4, 4), QUARTER)]
-
-    t_copy = copy(quarter(t_hbm, y), quarter(t_far, y), t_send, t_recv, mirror)
-
-    def y_copy(n):
-        block = quarter(t_far, y)
-        return copy(block, block, y_send.at[n], y_recv.at[n], column[n])
-
-    def y_wait(n):
-        block = quarter(t_far, y + (-1, 1, 2)[n])
-        copy(block, block, y_send.at[n], y_recv.at[n], column[n]).wait_recv()
+    def piece(ref, part, p):
+        return ref.at[pl.ds(QUARTER * lax.rem(part + 4, 4) + PIECE * p, PIECE)]
+
+    def t_copy(p):
+        return copy(piece(t_hbm, y, p), piece(t_far, y, p), t_send.at[p], t_recv.at[p], mirror)
+
+    def y_copy(p, n):
+        block = piece(t_far, y, p)
+        return copy(block, block, y_send.at[p, n], y_recv.at[p, n], column[n])
+
+    def y_pass(p):
+        t_copy(p).wait_recv()
+        for n in (2, 0, 1):
+            y_copy(p, n).start()
+
+    def y_build(p):
+        for n in range(3):
+            part = y + (-1, 1, 2)[n]
+            block = piece(t_far, part, p)
+            copy(block, block, y_send.at[p, n], y_recv.at[p, n], column[n]).wait_recv()
+            build_toeplitz(t_far, tz_far, wcol_far, QUARTER * lax.rem(part + 4, 4) + PIECE * p, PIECE)
 
     n_copy = copy(n_out, n_in, n_send, n_recv, mirror)
     r_copy = copy(r_out, r_in, r_send, r_recv, partner)
 
-    t_copy.start()
+    for p in range(3):
+        t_copy(p).start()
     h_start(0)
     for n in (2, 0, 1):
         x_copy(0, n).start()
@@ -277,30 +298,30 @@
     for n in range(2):
         x_copy(1, n).start()
     s_copy(1, 0).start()
+    y_pass(0)
     x_wait(0, 2)
     h_start(1)
     s_copy(0, 3).start()
-    t_copy.wait_recv()
-    for n in range(3):
-        y_copy(n).start()
+    y_pass(1)
     for n in range(2):
         x_wait(0, n)
         s_copy(0, 1 + n).start()
+    y_pass(2)
     build_toeplitz(t_far, tz_far, wcol_far, QUARTER * y, QUARTER)
     n_copy.wait_recv()
     got = n_in[...].astype(f32)
     choose(jnp.transpose(got[0:8] * 16.0 + got[8:16])[0:TRACES, 0:1], ids, TRACES)
+    y_build(0)
     h_wait(1)
     s_copy(1, 3).start()
     for n in range(2):
         x_wait(1, n)
         s_copy(1, 1 + n).start()
+    y_build(1)
     s_wait(0)
     xs[:, :TIME] = pick(ids[...], gm, 0, 5)
     band = band_matrix()
-    for n in range(3):
-        y_wait(n)
-        build_toeplitz(t_far, tz_far, wcol_far, QUARTER * lax.rem(y + (3, 1, 2)[n], 4), QUARTER)
+    y_build(2)
     s_wait(1)
     xs[pl.ds(TRACES, TRACES), TIME:] = pick(ids[pl.ds(TRACES, TRACES), :], gh, 0, 5)
     spread(xs, wb, TRACES)
@@ -308,6 +329,11 @@
     acc = jnp.zeros((96, LANES), f32)
     acc = correlate(tz_far, wb, sc, wcol_far, TRACES, 0, GROUPS, acc, 36)
     r_out[...] = fold(acc)
+
+    @pl.when(first_half)
+    def _():
+        pl.semaphore_wait(meet, 1)
+
     r_copy.start()
     xs[pl.ds(0, TRACES), TIME:] = pick(ids[pl.ds(0, TRACES), :], gh, 0, 5)
     spread(xs, wb, 0)
@@ -317,15 +343,18 @@
     sums[...] = total + r_in[...]
     finish(sums, mcol, o_ref)
 
+    for p in range(3):
+        t_copy(p).wait_send()
+        for n in range(3):
+            y_copy(p, n).wait_send()
     for n in range(3):
-        y_copy(n).wait_send()
         x_copy(0, n).wait_send()
     for n in range(2):
         x_copy(1, n).wait_send()
     for n in range(4):
         for s in range(2):
             s_copy(s, n).wait_send()
-    for sent in (t_copy, n_copy, r_copy):
+    for sent in (n_copy, r_copy):
         sent.wait_send()
 
     @pl.when(has_earlier)
@@ -376,14 +405,15 @@
             dma((2, 4)),
             dma((2,)),
             dma((2,)),
-            dma,
-            dma,
             dma((3,)),
             dma((3,)),
+            dma((3, 3)),
+            dma((3, 3)),
             dma,
             dma,
             dma,
             dma,
+            pltpu.SemaphoreType.REGULAR,
         ],
         compiler_params=pltpu.CompilerParams(
             collective_id=0, has_side_effects=True, vmem_limit_bytes=56 * 2**20

time: 40.9 us -> 40.4 us (0.988)
  Pallas kernels: 39.4 us -> 38.9 us
    pallas_call x1, Pallas kernels: 39.4 us -> 38.9 us  [per_device(): pl.pallas_call(kernel, out_shape=jax.ShapeDtypeStruct((MEMBERS, TIME), f3...]
where the time goes in v5:
time: 40.4 us; the launch traced here: 40.2 us
  Pallas kernels  38.9 us (96%)
  local copies, waits for them, and re-layouts  1.3 us (3%)
    pallas_call x1, Pallas kernels, per_device(): pl.pallas_call(kernel, out_shape=jax.ShapeDtypeStruct((MEMBERS, TIME), f3...  38.9 us
    unnamed x1, local copies, waits for them, and re-layouts  1.3 us

profile of v5, /device:TPU:24, one launch (start us, length us, event | category | flops | bytes accessed | tf_op | source)
XLA Modules:
  0.0 40.2 jit_solution(6533049460024917120)
XLA Ops:
  0.0 38.9 %shard_map.46 = f32[4,640]{1,0:T(4,128)} custom-call(bf16[3,25,640]{2,1,0:T(8,128)(2,1)} %bitcast.6, bf16[36,4,600]{2,1,0:T(4,128)(2,1)} %bitcast.5, s32[4,12]{1,0:T(4,128)} %idx_hbm.1, s32[3,4,12]{2,1,0:T(4,128)} %bitcast.7), custom_call_target="tpu_custom_call" | custom-call | tf_op jit(solution)/shard_map/pallas_call | solution.py:372
  38.9 1.3 %copy.6 = f32[4,640]{1,0:T(4,128)} copy(f32[4,640]{1,0:T(4,128)} %shard_map.46) | data formatting | bytes 20480

commit v6 on v5

--- a/solution.py
+++ b/solution.py
@@ -165,8 +165,7 @@
             ((w_hbm, w_ref), (idx_hbm, idx_ref), (mask_hbm, mask_ref), (t_hbm, t_ref))
         )
     ]
-    for load in loads:
-        load.start()
+    loads[0].start()
 
     other = (1 - zh) * 8 + at(x, core)
     partner = (other, tm)
@@ -178,7 +177,7 @@
     has_earlier, has_later = tm > 0, tm < 31
 
     barrier = pltpu.get_barrier_semaphore()
-    friends = (*across, *column, sibling, mirror)
+    friends = (mirror, *across, *column, sibling)
     for friend in friends:
         pl.semaphore_signal(barrier, inc=1, device_id=friend, device_id_type=MESH)
 
@@ -196,6 +195,8 @@
     def _():
         pl.semaphore_signal(barrier, inc=1, device_id=later, device_id_type=MESH)
 
+    for load in loads[1:]:
+        load.start()
     loads[0].wait()
     own = w_ref[...].astype(f32)
     packed = jnp.concatenate([own[0], own[1], own[2], jnp.zeros((ROWS - 3 * PER, TIME), f32)], axis=0)
@@ -294,19 +295,19 @@
     choose(mine[0:TRACES, 0:1], ids, 0)
     loads[3].wait()
     build_toeplitz(t_ref, tz, wcol, 0, GROUPS)
+    y_pass(0)
     h_wait(0)
     for n in range(2):
         x_copy(1, n).start()
     s_copy(1, 0).start()
-    y_pass(0)
     x_wait(0, 2)
     h_start(1)
     s_copy(0, 3).start()
     y_pass(1)
+    y_pass(2)
     for n in range(2):
         x_wait(0, n)
         s_copy(0, 1 + n).start()
-    y_pass(2)
     build_toeplitz(t_far, tz_far, wcol_far, QUARTER * y, QUARTER)
     n_copy.wait_recv()
     got = n_in[...].astype(f32)

time: 40.4 us -> 40.3 us (level)
  no operation moved by 1% of the time
where the time goes in v6:
time: 40.3 us; the launch traced here: 40.2 us
  Pallas kernels  38.9 us (97%)
  local copies, waits for them, and re-layouts  1.3 us (3%)
    pallas_call x1, Pallas kernels, per_device(): pl.pallas_call(kernel, out_shape=jax.ShapeDtypeStruct((MEMBERS, TIME), f3...  38.9 us
    unnamed x1, local copies, waits for them, and re-layouts  1.3 us

profile of v6, /device:TPU:24, one launch (start us, length us, event | category | flops | bytes accessed | tf_op | source)
XLA Modules:
  0.0 40.2 jit_solution(1937523546362578954)
XLA Ops:
  0.0 38.9 %shard_map.46 = f32[4,640]{1,0:T(4,128)} custom-call(bf16[3,25,640]{2,1,0:T(8,128)(2,1)} %bitcast.6, bf16[36,4,600]{2,1,0:T(4,128)(2,1)} %bitcast.5, s32[4,12]{1,0:T(4,128)} %idx_hbm.1, s32[3,4,12]{2,1,0:T(4,128)} %bitcast.7), custom_call_target="tpu_custom_call" | custom-call | tf_op jit(solution)/shard_map/pallas_call | solution.py:373
  38.9 1.3 %copy.6 = f32[4,640]{1,0:T(4,128)} copy(f32[4,640]{1,0:T(4,128)} %shard_map.46) | data formatting | bytes 20480

commit v7 on v6

--- a/solution.py
+++ b/solution.py
@@ -339,7 +339,7 @@
     xs[pl.ds(0, TRACES), TIME:] = pick(ids[pl.ds(0, TRACES), :], gh, 0, 5)
     spread(xs, wb, 0)
     window_scales(xs, band, sc, 0)
-    total = fold(correlate(tz, wb, sc, wcol, 0, 0, GROUPS, jnp.zeros((96, LANES), f32), 12))
+    total = fold(correlate(tz, wb, sc, wcol, 0, 0, GROUPS, jnp.zeros((96, LANES), f32), 36))
     r_copy.wait_recv()
     sums[...] = total + r_in[...]
     finish(sums, mcol, o_ref)

time: 40.3 us -> 40.2 us (level)
  no operation moved by 1% of the time
where the time goes in v7:
time: 40.2 us; the launch traced here: 40 us
  Pallas kernels  38.7 us (96%)
  local copies, waits for them, and re-layouts  1.3 us (3%)
    pallas_call x1, Pallas kernels, per_device(): pl.pallas_call(kernel, out_shape=jax.ShapeDtypeStruct((MEMBERS, TIME), f3...  38.7 us
    unnamed x1, local copies, waits for them, and re-layouts  1.3 us

profile of v7, /device:TPU:24, one launch (start us, length us, event | category | flops | bytes accessed | tf_op | source)
XLA Modules:
  0.0 40.0 jit_solution(5579154747198855101)
XLA Ops:
  0.0 38.7 %shard_map.46 = f32[4,640]{1,0:T(4,128)} custom-call(bf16[3,25,640]{2,1,0:T(8,128)(2,1)} %bitcast.6, bf16[36,4,600]{2,1,0:T(4,128)(2,1)} %bitcast.5, s32[4,12]{1,0:T(4,128)} %idx_hbm.1, s32[3,4,12]{2,1,0:T(4,128)} %bitcast.7), custom_call_target="tpu_custom_call" | custom-call | tf_op jit(solution)/shard_map/pallas_call | solution.py:373
  38.7 1.3 %copy.6 = f32[4,640]{1,0:T(4,128)} copy(f32[4,640]{1,0:T(4,128)} %shard_map.46) | data formatting | bytes 20480
